TPU v7x, 256 devices: a whole 4x4x8 slice. The times are simulated.
256 devices in a mesh: cluster: 8 (over y, core), sub: 32 (over x, z).
Axes of the slice: x: 4, y: 4, z: 8, core: 2. Of those that a mesh axis runs over, the one named last changes fastest.
Arguments:
- compliance: float32 [8, 32, 1024, 1024], P('cluster', 'sub'), may hold values from -0.078125 to 4.078125, as said below
- loads: float32 [8, 32, 1024, 256], P('cluster', 'sub'), may hold values from -6 to 6
- modes: float32 [8, 32, 32, 1024], P('cluster', 'sub'), may hold values from -1 to 1
- coarse_inverse: float32 [8, 1024, 1024], P('cluster', 'sub'), may hold values from -0.9 to 0.9, as said below
- face_block: int32 [8, 32, 4], replicated, may hold values from 0 to 7, as said below
- edge_rows: int32 [8, 32, 2], replicated, may hold values from 16 to 128
Outputs:
- solution: float32 [8, 32, 1024, 256], P('cluster', 'sub')
- residual: float32 [8, 32, 1024, 256], P('cluster', 'sub')
Inputs may be any that keep to these rules, and one draw needn't show every extreme that they name: `compliance`: symmetric positive definite for every subdomain. `coarse_inverse`: symmetric positive definite for every cluster. `face_block`: the four faces of a subdomain lie in four different row blocks. `edge_rows`: entries of faces with no partner are not read.
All inputs are finite; a program needn't handle non-finite values.
Results may differ from a plain program's by a relative error of at most 0.00018.
Values sent between devices are 32-bit elements; how exact they have to be, the bound alone decides.
A program may use at most 64 MiB of HBM per device.

v0:
```python
import jax
import jax.numpy as jnp
from jax import lax
from jax.sharding import Mesh
from jax.sharding import PartitionSpec as P

BLOCK = 128
ITERS = 3
SUB = ("sub_0", "sub_1")
CLUSTER = ("cluster_0", "cluster_1")
CLUSTER_SUB = ("cluster_0", "cluster_1", "sub_0", "sub_1")


def from_behind(value, axis, steps):
    count = lax.axis_size(axis)
    initial, last = (max(0, -steps), min(count, count - steps))
    return lax.ppermute(value, axis, [(source, source + steps) for source in range(initial, last)])


def copy_for_each(x, axis):
    copies = jnp.broadcast_to(x, (lax.axis_size(axis), *x.shape))
    return lax.all_to_all(copies, axis, split_axis=0, concat_axis=0, tiled=True)


def in_order(parts, dim):
    shape = list(parts.shape[1:])
    shape[dim] *= parts.shape[0]
    return jnp.moveaxis(parts, 0, dim).reshape(shape)


def collect(x, axis, dim):
    parts = copy_for_each(x, axis)
    return in_order(parts, dim)


def one_axis_at_a_time(x, axes):
    for axis in axes:
        x = lax.psum(x, axis)
    return x


def take_block(field, block_index):
    return lax.dynamic_slice_in_dim(field, block_index * BLOCK, BLOCK, 0)


def add_block(field, block_index, arrived, length):
    rows = jnp.arange(BLOCK, dtype=jnp.int32)
    weight = (0.5 * (rows < length).astype(jnp.float32))[:, None]
    current = take_block(field, block_index)
    return lax.dynamic_update_slice_in_dim(
        field, current + weight * arrived, block_index * BLOCK, 0
    )


def assemble(field, faces, sub_routes, clus_routes):
    result = field
    for send_face, recv_face, length, offset in sub_routes:
        arrived = from_behind(take_block(field, faces[send_face]), SUB, offset)
        result = add_block(result, faces[recv_face], arrived, length)
    for send_face, recv_face, length, offset in clus_routes:
        arrived = from_behind(take_block(field, faces[send_face]), CLUSTER, offset)
        result = add_block(result, faces[recv_face], arrived, length)
    return result


def precondition(basis, inverse_rows, resid):
    coarse = jnp.dot(basis, resid, precision=lax.Precision.HIGHEST)
    solved = jnp.dot(inverse_rows, collect(coarse, SUB, 0), precision=lax.Precision.HIGHEST)
    return resid + jnp.einsum("mo,ml->ol", basis, solved, precision=lax.Precision.HIGHEST)


def paired_dots(first, second, third):
    return (
        one_axis_at_a_time(jnp.sum(first * second, axis=0), CLUSTER_SUB),
        one_axis_at_a_time(jnp.sum(third * second, axis=0), CLUSTER_SUB),
    )


def shards(compliance, loads, modes, coarse_inverse, face_block, edge_rows):
    matrix = compliance[0, 0]
    rhs = loads[0, 0]
    basis = modes[0, 0]
    inverse_rows = coarse_inverse[0]
    clus_index = lax.axis_index(CLUSTER)
    sub_index = lax.axis_index(SUB)
    faces = face_block[clus_index, sub_index]
    sub_low = edge_rows[clus_index, jnp.maximum(sub_index - 1, 0), 0]
    sub_high = edge_rows[clus_index, sub_index, 0]
    clus_low = edge_rows[jnp.maximum(clus_index - 1, 0), sub_index, 1]
    clus_high = edge_rows[clus_index, sub_index, 1]
    sub_routes = ((1, 0, sub_low, 1), (0, 1, sub_high, -1))
    clus_routes = ((3, 2, clus_low, 1), (2, 3, clus_high, -1))

    def operator(field):
        inner = assemble(field, faces, sub_routes, clus_routes)
        product = jnp.dot(matrix, inner, precision=lax.Precision.HIGHEST)
        return assemble(product, faces, sub_routes, clus_routes)

    solution = jnp.zeros_like(rhs)
    residual = rhs
    precond = precondition(basis, inverse_rows, residual)
    image = operator(precond)
    rz_now, curve = paired_dots(residual, precond, image)
    alpha = rz_now / curve
    direction, along = (precond, image)
    for step in range(ITERS):
        solution = solution + alpha * direction
        residual = residual - alpha * along
        if step + 1 < ITERS:
            precond = precondition(basis, inverse_rows, residual)
            image = operator(precond)
            rz_next, curve = paired_dots(residual, precond, image)
            ratio = rz_next / rz_now
            alpha = rz_next / (curve - ratio * rz_next / alpha)
            direction = precond + ratio * direction
            along = image + ratio * along
            rz_now = rz_next
    return (solution[None, None], residual[None, None])


def solution(mesh):
    finer = Mesh(mesh.devices.reshape(4, 2, 4, 8), ("cluster_0", "cluster_1", "sub_0", "sub_1"))
    in_specs = (
        P(CLUSTER, SUB, None, None),
        P(CLUSTER, SUB, None, None),
        P(CLUSTER, SUB, None, None),
        P(CLUSTER, SUB, None),
        P(),
        P(),
    )
    out_specs = (P(CLUSTER, SUB, None, None), P(CLUSTER, SUB, None, None))
    return jax.shard_map(
        shards, mesh=finer, in_specs=in_specs, out_specs=out_specs, check_vma=False
    )
```

profile of v0, /device:TPU:2, one launch (start us, length us, event | category | flops | bytes accessed | tf_op | source)
XLA Modules:
  0.0 355.4 jit_solution(10099001294566867141)
XLA Ops:
  4.4 11.6 %all-to-all-start = ((f32[32,32,256]{2,1,0:T(8,128)}), f32[32,32,256]{2,1,0:T(8,128)S(1)}, u32[]{:S(2)}, u32[]{:S(2)}) async-start(f32[32,32,256]{2,1,0:T(8,128)} %broadcast_in_dim.10), calls=%async_computation | async-start | bytes 2097152 | tf_op jit(solution)/shard_map/all_to_all | solution.py:22
  20.0 22.2 %all-to-all-done = f32[32,32,256]{2,1,0:T(8,128)S(1)} async-done(((f32[32,32,256]{2,1,0:T(8,128)}), f32[32,32,256]{2,1,0:T(8,128)S(1)}, u32[]{:S(2)}, u32[]{:S(2)}) %all-to-all-start) | async-done | bytes 1048608 | tf_op jit(solution)/shard_map/all_to_all | solution.py:22
  45.0 5.0 %collective-permute-start = (f32[128,256]{0,1:T(8,128)S(1)}, f32[128,256]{0,1:T(8,128)}, u32[]{:S(2)}, u32[]{:S(2)}) collective-permute-start(f32[128,256]{0,1:T(8,128)S(1)} %constant_dynamic-slice_fusion.11), channel_id=1, source_target_pairs={{0,1},{1,2},{2,3},{3,4},{4,5},{5,6},{6,7},{7,8},{8,9},{9,10},{10,1... | collective-permute-start | bytes 393224 | tf_op jit(solution)/shard_map/ppermute | solution.py:17
  64.6 3.7 %fusion.4 = f32[256,1024]{1,0:T(8,128)S(1)} fusion(f32[1024,256]{0,1:T(8,128)S(1)} %add_dynamic-update-slice_fusion.20, f32[1,1,1024,1024]{3,2,1,0:T(8,128)S(1)} %copy-done.1), kind=kOutput, calls=%fused_computation.4 | convolution fusion | flops 3221225472 | bytes 6291456 | tf_op jit(solution)/shard_map/dot_general | solution.py:96
  68.4 3.0 collective-permute-start.4
  72.8 4.4 %collective-permute-start.6 = (f32[128,256]{0,1:T(8,128)S(1)}, f32[128,256]{0,1:T(8,128)S(1)}, u32[]{:S(2)}, u32[]{:S(2)}) collective-permute-start(f32[128,256]{0,1:T(8,128)S(1)} %get-tuple-element.56), channel_id=1, source_target_pairs={{0,32},{32,64},{64,96},{96,128},{128,160},{160,192},{192,224},{1,3... | collective-permute-start | bytes 393224 | tf_op jit(solution)/shard_map/ppermute | solution.py:17
  77.2 4.9 %collective-permute-start.5 = (f32[128,256]{0,1:T(8,128)S(1)}, f32[128,256]{0,1:T(8,128)S(1)}, u32[]{:S(2)}, u32[]{:S(2)}) collective-permute-start(f32[128,256]{0,1:T(8,128)S(1)} %get-tuple-element.58), channel_id=1, source_target_pairs={{1,0},{2,1},{3,2},{4,3},{5,4},{6,5},{7,6},{8,7},{9,8},{10,9},{11,1... | collective-permute-start | bytes 393224 | tf_op jit(solution)/shard_map/ppermute | solution.py:17
  85.1 12.3 %all-reduce.8 = (f32[256]{0:T(256)S(1)}, f32[256]{0:T(256)S(1)}) all-reduce(f32[256]{0:T(256)S(1)} %get-tuple-element.9, f32[256]{0:T(256)S(1)} %get-tuple-element.8), channel_id=1, replica_groups=mesh['cluster_0'=4,'cluster_1'=2,'sub_0'=4,'sub_1'=8] {'cluster_0'}, use_global_device_ids=true, to_apply=%region_1.0 | all-reduce | flops 512 | bytes 4096 | tf_op jit(solution)/shard_map/psum | solution.py:38
  99.8 8.7 %all-reduce.5 = (f32[256]{0:T(256)S(1)}, f32[256]{0:T(256)S(1)}) all-reduce(f32[256]{0:T(256)S(1)} %get-tuple-element.32, f32[256]{0:T(256)S(1)} %get-tuple-element.33), channel_id=1, replica_groups=mesh['cluster_0'=4,'cluster_1'=2,'sub_0'=4,'sub_1'=8] {'sub_0'}, use_global_device_ids=true, to_apply=%region_3.0 | all-reduce | flops 512 | bytes 4096 | tf_op jit(solution)/shard_map/psum | solution.py:38
  108.5 18.3 %all-reduce.2 = (f32[256]{0:T(256)S(1)}, f32[256]{0:T(256)S(1)}) all-reduce(f32[256]{0:T(256)S(1)} %get-tuple-element.20, f32[256]{0:T(256)S(1)} %get-tuple-element.21), channel_id=1, replica_groups=mesh['cluster_0'=4,'cluster_1'=2,'sub_0'=4,'sub_1'=8] {'sub_1'}, use_global_device_ids=true, to_apply=%region_4.0 | all-reduce | flops 512 | bytes 4096 | tf_op jit(solution)/shard_map/psum | solution.py:38
  129.3 25.4 %all_to_all.15 = f32[32,32,256]{2,1,0:T(8,128)S(1)} all-to-all(f32[32,32,256]{2,1,0:T(8,128)S(1)} %broadcast_in_dim.11), channel_id=1, replica_groups=mesh['cluster_0'=4,'cluster_1'=2,'sub_0'=4,'sub_1'=8] {'sub_0','sub_1'}, dimensions={0} | all-to-all | bytes 2097152 | tf_op jit(solution)/shard_map/all_to_all | solution.py:22
  157.5 5.5 %collective-permute-start.8 = (f32[128,256]{0,1:T(8,128)S(1)}, f32[128,256]{0,1:T(8,128)S(1)}, u32[]{:S(2)}, u32[]{:S(2)}) collective-permute-start(f32[128,256]{0,1:T(8,128)S(1)} %constant_dynamic-slice_fusion.4), channel_id=1, source_target_pairs={{0,1},{1,2},{2,3},{3,4},{4,5},{5,6},{6,7},{7,8},{8,9},{9,10},{10,1... | collective-permute-start | bytes 393224 | tf_op jit(solution)/shard_map/ppermute | solution.py:17
  163.1 3.4 collective-permute-done.8
  166.6 3.2 collective-permute-start.9
  175.2 3.7 %fusion.2 = f32[256,1024]{1,0:T(8,128)S(1)} fusion(f32[1024,256]{0,1:T(8,128)S(1)} %add_dynamic-update-slice_fusion.12, f32[1,1,1024,1024]{3,2,1,0:T(8,128)S(1)} %copy-done.2), kind=kOutput, calls=%fused_computation.2 | convolution fusion | flops 3221225472 | bytes 6291456 | tf_op jit(solution)/shard_map/dot_general | solution.py:96
  183.0 3.7 %collective-permute-start.14 = (f32[128,256]{0,1:T(8,128)S(1)}, f32[128,256]{0,1:T(8,128)S(1)}, u32[]{:S(2)}, u32[]{:S(2)}) collective-permute-start(f32[128,256]{0,1:T(8,128)S(1)} %get-tuple-element.48), channel_id=1, source_target_pairs={{0,32},{32,64},{64,96},{96,128},{128,160},{160,192},{192,224},{1,3... | collective-permute-start | bytes 393224 | tf_op jit(solution)/shard_map/ppermute | solution.py:17
  186.7 5.3 %collective-permute-start.13 = (f32[128,256]{0,1:T(8,128)S(1)}, f32[128,256]{0,1:T(8,128)S(1)}, u32[]{:S(2)}, u32[]{:S(2)}) collective-permute-start(f32[128,256]{0,1:T(8,128)S(1)} %get-tuple-element.50), channel_id=1, source_target_pairs={{1,0},{2,1},{3,2},{4,3},{5,4},{6,5},{7,6},{8,7},{9,8},{10,9},{11,1... | collective-permute-start | bytes 393224 | tf_op jit(solution)/shard_map/ppermute | solution.py:17
  196.0 11.3 %all-reduce.7 = (f32[256]{0:T(256)S(1)}, f32[256]{0:T(256)S(1)}) all-reduce(f32[256]{0:T(256)S(1)} %get-tuple-element.7, f32[256]{0:T(256)S(1)} %get-tuple-element.6), channel_id=1, replica_groups=mesh['cluster_0'=4,'cluster_1'=2,'sub_0'=4,'sub_1'=8] {'cluster_0'}, use_global_device_ids=true, to_apply=%region_11.0 | all-reduce | flops 512 | bytes 4096 | tf_op jit(solution)/shard_map/psum | solution.py:38
  209.7 8.2 %all-reduce.4 = (f32[256]{0:T(256)S(1)}, f32[256]{0:T(256)S(1)}) all-reduce(f32[256]{0:T(256)S(1)} %get-tuple-element.30, f32[256]{0:T(256)S(1)} %get-tuple-element.31), channel_id=1, replica_groups=mesh['cluster_0'=4,'cluster_1'=2,'sub_0'=4,'sub_1'=8] {'sub_0'}, use_global_device_ids=true, to_apply=%region_13.0 | all-reduce | flops 512 | bytes 4096 | tf_op jit(solution)/shard_map/psum | solution.py:38
  217.9 18.8 %all-reduce.1 = (f32[256]{0:T(256)S(1)}, f32[256]{0:T(256)S(1)}) all-reduce(f32[256]{0:T(256)S(1)} %get-tuple-element.18, f32[256]{0:T(256)S(1)} %get-tuple-element.19), channel_id=1, replica_groups=mesh['cluster_0'=4,'cluster_1'=2,'sub_0'=4,'sub_1'=8] {'sub_1'}, use_global_device_ids=true, to_apply=%region_14.0 | all-reduce | flops 512 | bytes 4096 | tf_op jit(solution)/shard_map/psum | solution.py:38
  239.3 25.5 %all_to_all.16 = f32[32,32,256]{2,1,0:T(8,128)S(1)} all-to-all(f32[32,32,256]{2,1,0:T(8,128)S(1)} %broadcast_in_dim.12), channel_id=1, replica_groups=mesh['cluster_0'=4,'cluster_1'=2,'sub_0'=4,'sub_1'=8] {'sub_0','sub_1'}, dimensions={0} | all-to-all | bytes 2097152 | tf_op jit(solution)/shard_map/all_to_all | solution.py:22
  267.7 5.5 %collective-permute-start.16 = (f32[128,256]{0,1:T(8,128)S(1)}, f32[128,256]{0,1:T(8,128)S(1)}, u32[]{:S(2)}, u32[]{:S(2)}) collective-permute-start(f32[128,256]{0,1:T(8,128)S(1)} %constant_dynamic-slice_fusion), channel_id=1, source_target_pairs={{0,1},{1,2},{2,3},{3,4},{4,5},{5,6},{6,7},{7,8},{8,9},{9,10},{10,1... | collective-permute-start | bytes 393224 | tf_op jit(solution)/shard_map/ppermute | solution.py:17
  273.3 3.4 collective-permute-done.16
  276.7 3.2 collective-permute-start.17
  281.2 3.3 collective-permute-start.18
  285.3 3.7 %fusion = f32[256,1024]{1,0:T(8,128)S(1)} fusion(f32[1024,256]{0,1:T(8,128)S(1)} %add_dynamic-update-slice_fusion.4, f32[1,1,1024,1024]{3,2,1,0:T(8,128)S(1)} %copy-done.3), kind=kOutput, calls=%fused_computation | convolution fusion | flops 3221225472 | bytes 6291456 | tf_op jit(solution)/shard_map/dot_general | solution.py:96
  293.3 3.3 collective-permute-start.22
  296.5 5.3 %collective-permute-start.21 = (f32[128,256]{0,1:T(8,128)S(1)}, f32[128,256]{0,1:T(8,128)S(1)}, u32[]{:S(2)}, u32[]{:S(2)}) collective-permute-start(f32[128,256]{0,1:T(8,128)S(1)} %get-tuple-element.42), channel_id=1, source_target_pairs={{1,0},{2,1},{3,2},{4,3},{5,4},{6,5},{7,6},{8,7},{9,8},{10,9},{11,1... | collective-permute-start | bytes 393224 | tf_op jit(solution)/shard_map/ppermute | solution.py:17
  305.5 11.2 %all-reduce.6 = (f32[256]{0:T(256)S(1)}, f32[256]{0:T(256)S(1)}) all-reduce(f32[256]{0:T(256)S(1)} %get-tuple-element.5, f32[256]{0:T(256)S(1)} %get-tuple-element.4), channel_id=1, replica_groups=mesh['cluster_0'=4,'cluster_1'=2,'sub_0'=4,'sub_1'=8] {'cluster_0'}, use_global_device_ids=true, to_apply=%region_21.0 | all-reduce | flops 512 | bytes 4096 | tf_op jit(solution)/shard_map/psum | solution.py:38
  319.1 8.2 %all-reduce.3 = (f32[256]{0:T(256)S(1)}, f32[256]{0:T(256)S(1)}) all-reduce(f32[256]{0:T(256)S(1)} %get-tuple-element.28, f32[256]{0:T(256)S(1)} %get-tuple-element.29), channel_id=1, replica_groups=mesh['cluster_0'=4,'cluster_1'=2,'sub_0'=4,'sub_1'=8] {'sub_0'}, use_global_device_ids=true, to_apply=%region_23.0 | all-reduce | flops 512 | bytes 4096 | tf_op jit(solution)/shard_map/psum | solution.py:38
  327.4 18.8 %all-reduce = (f32[256]{0:T(256)S(1)}, f32[256]{0:T(256)S(1)}) all-reduce(f32[256]{0:T(256)S(1)} %get-tuple-element.16, f32[256]{0:T(256)S(1)} %get-tuple-element.17), channel_id=1, replica_groups=mesh['cluster_0'=4,'cluster_1'=2,'sub_0'=4,'sub_1'=8] {'sub_1'}, use_global_device_ids=true, to_apply=%region_24.0 | all-reduce | flops 512 | bytes 4096 | tf_op jit(solution)/shard_map/psum | solution.py:38
  346.1 4.1 %subtract_bitcast_fusion = (f32[1,1,1024,256]{2,3,1,0:T(8,128)}, f32[1,1,1024,256]{2,3,1,0:T(8,128)}) fusion(f32[1024,256]{0,1:T(8,128)S(1)} %multiply_subtract_fusion, f32[1024,256]{0,1:T(8,128)} %copy-done.10, f32[256]{0:T(256)S(1)} %get-tuple-element.35, f32[256]{0:T(256)S(1)} %get-tuple-element.34, f32[1024,256]{0,1:T(8,128)S(1)} %copy-done.5, ...), kind=kLoop, calls=%fused_computation.19 | loop fusion | flops 3932160 | bytes 9442304 | tf_op jit(solution)/shard_map/broadcast_in_dim | solution.py:118
  (128 shorter events, 73.3 us)
Async XLA Ops:
  0.7 41.5 %copy-start.12 = (f32[1,32,1024]{2,1,0:T(8,128)S(1)}, f32[1,32,1024]{2,1,0:T(8,128)}, u32[]{:S(2)}) copy-start(f32[1,32,1024]{2,1,0:T(8,128)} %param.9) | copy-start | bytes 393220
  4.4 37.7 %all-to-all-start = ((f32[32,32,256]{2,1,0:T(8,128)}), f32[32,32,256]{2,1,0:T(8,128)S(1)}, u32[]{:S(2)}, u32[]{:S(2)}) async-start(f32[32,32,256]{2,1,0:T(8,128)} %broadcast_in_dim.10), calls=%async_computation | async-start | bytes 2097152 | tf_op jit(solution)/shard_map/all_to_all | solution.py:22
  16.4 68.3 %copy-start.9 = (f32[1,1,1024,256]{2,3,1,0:T(8,128)}, f32[1,1,1024,256]{2,3,1,0:T(8,128)S(1)}, u32[]{:S(2)}) copy-start(f32[1,1,1024,256]{2,3,1,0:T(8,128)S(1)} %copy.8) | copy-start | bytes 3145732
  44.9 39.8 %copy-start.6 = (f32[1024,256]{0,1:T(8,128)}, f32[1024,256]{0,1:T(8,128)S(1)}, u32[]{:S(2)}) copy-start(f32[1024,256]{0,1:T(8,128)S(1)} %fusion.8) | copy-start | bytes 3145732
  45.0 9.1 %collective-permute-start = (f32[128,256]{0,1:T(8,128)S(1)}, f32[128,256]{0,1:T(8,128)}, u32[]{:S(2)}, u32[]{:S(2)}) collective-permute-start(f32[128,256]{0,1:T(8,128)S(1)} %constant_dynamic-slice_fusion.11), channel_id=1, source_target_pairs={{0,1},{1,2},{2,3},{3,4},{4,5},{5,6},{6,7},{7,8},{8,9},{9,10},{10,1... | collective-permute-start | bytes 393224 | tf_op jit(solution)/shard_map/ppermute | solution.py:17
  55.0 8.5 %collective-permute-start.1 = (f32[128,256]{0,1:T(8,128)S(1)}, f32[128,256]{0,1:T(8,128)S(1)}, u32[]{:S(2)}, u32[]{:S(2)}) collective-permute-start(f32[128,256]{0,1:T(8,128)S(1)} %get-tuple-element.62), channel_id=1, source_target_pairs={{1,0},{2,1},{3,2},{4,3},{5,4},{6,5},{7,6},{8,7},{9,8},{10,9},{11,1... | collective-permute-start | bytes 393224 | tf_op jit(solution)/shard_map/ppermute | solution.py:17
  59.2 5.3 %collective-permute-start.3 = (f32[128,256]{0,1:T(8,128)S(1)}, f32[128,256]{0,1:T(8,128)S(1)}, u32[]{:S(2)}, u32[]{:S(2)}) collective-permute-start(f32[128,256]{0,1:T(8,128)S(1)} %get-tuple-element.59), channel_id=1, source_target_pairs={{32,0},{64,32},{96,64},{128,96},{160,128},{192,160},{224,192},{33,... | collective-permute-start | bytes 393224 | tf_op jit(solution)/shard_map/ppermute | solution.py:17
  60.5 4.0 %collective-permute-start.2 = (f32[128,256]{0,1:T(8,128)S(1)}, f32[128,256]{0,1:T(8,128)S(1)}, u32[]{:S(2)}, u32[]{:S(2)}) collective-permute-start(f32[128,256]{0,1:T(8,128)S(1)} %get-tuple-element.60), channel_id=1, source_target_pairs={{0,32},{32,64},{64,96},{96,128},{128,160},{160,192},{192,224},{1,3... | collective-permute-start | bytes 393224 | tf_op jit(solution)/shard_map/ppermute | solution.py:17
  68.4 13.8 %collective-permute-start.4 = (f32[128,256]{0,1:T(8,128)S(1)}, f32[128,256]{0,1:T(8,128)S(1)}, u32[]{:S(2)}, u32[]{:S(2)}) collective-permute-start(f32[128,256]{0,1:T(8,128)S(1)} %get-tuple-element.57), channel_id=1, source_target_pairs={{0,1},{1,2},{2,3},{3,4},{4,5},{5,6},{6,7},{7,8},{8,9},{9,10},{10,1... | collective-permute-start | bytes 393224 | tf_op jit(solution)/shard_map/ppermute | solution.py:17
  71.5 13.2 %collective-permute-start.7 = (f32[128,256]{0,1:T(8,128)S(1)}, f32[128,256]{0,1:T(8,128)S(1)}, u32[]{:S(2)}, u32[]{:S(2)}) collective-permute-start(f32[128,256]{0,1:T(8,128)S(1)} %get-tuple-element.55), channel_id=1, source_target_pairs={{32,0},{64,32},{96,64},{128,96},{160,128},{192,160},{224,192},{33,... | collective-permute-start | bytes 393224 | tf_op jit(solution)/shard_map/ppermute | solution.py:17
  72.8 11.9 %collective-permute-start.6 = (f32[128,256]{0,1:T(8,128)S(1)}, f32[128,256]{0,1:T(8,128)S(1)}, u32[]{:S(2)}, u32[]{:S(2)}) collective-permute-start(f32[128,256]{0,1:T(8,128)S(1)} %get-tuple-element.56), channel_id=1, source_target_pairs={{0,32},{32,64},{64,96},{96,128},{128,160},{160,192},{192,224},{1,3... | collective-permute-start | bytes 393224 | tf_op jit(solution)/shard_map/ppermute | solution.py:17
  77.2 7.4 %collective-permute-start.5 = (f32[128,256]{0,1:T(8,128)S(1)}, f32[128,256]{0,1:T(8,128)S(1)}, u32[]{:S(2)}, u32[]{:S(2)}) collective-permute-start(f32[128,256]{0,1:T(8,128)S(1)} %get-tuple-element.58), channel_id=1, source_target_pairs={{1,0},{2,1},{3,2},{4,3},{5,4},{6,5},{7,6},{8,7},{9,8},{10,9},{11,1... | collective-permute-start | bytes 393224 | tf_op jit(solution)/shard_map/ppermute | solution.py:17
  157.5 37.2 %copy-start.7 = (f32[1024,256]{0,1:T(8,128)}, f32[1024,256]{0,1:T(8,128)S(1)}, u32[]{:S(2)}) copy-start(f32[1024,256]{0,1:T(8,128)S(1)} %fusion.7) | copy-start | bytes 3145732
  157.5 9.0 %collective-permute-start.8 = (f32[128,256]{0,1:T(8,128)S(1)}, f32[128,256]{0,1:T(8,128)S(1)}, u32[]{:S(2)}, u32[]{:S(2)}) collective-permute-start(f32[128,256]{0,1:T(8,128)S(1)} %constant_dynamic-slice_fusion.4), channel_id=1, source_target_pairs={{0,1},{1,2},{2,3},{3,4},{4,5},{5,6},{6,7},{7,8},{8,9},{9,10},{10,1... | collective-permute-start | bytes 393224 | tf_op jit(solution)/shard_map/ppermute | solution.py:17
  166.6 7.6 %collective-permute-start.9 = (f32[128,256]{0,1:T(8,128)S(1)}, f32[128,256]{0,1:T(8,128)S(1)}, u32[]{:S(2)}, u32[]{:S(2)}) collective-permute-start(f32[128,256]{0,1:T(8,128)S(1)} %get-tuple-element.54), channel_id=1, source_target_pairs={{1,0},{2,1},{3,2},{4,3},{5,4},{6,5},{7,6},{8,7},{9,8},{10,9},{11,1... | collective-permute-start | bytes 393224 | tf_op jit(solution)/shard_map/ppermute | solution.py:17
  169.8 5.3 %collective-permute-start.11 = (f32[128,256]{0,1:T(8,128)S(1)}, f32[128,256]{0,1:T(8,128)S(1)}, u32[]{:S(2)}, u32[]{:S(2)}) collective-permute-start(f32[128,256]{0,1:T(8,128)S(1)} %get-tuple-element.51), channel_id=1, source_target_pairs={{32,0},{64,32},{96,64},{128,96},{160,128},{192,160},{224,192},{33,... | collective-permute-start | bytes 393224 | tf_op jit(solution)/shard_map/ppermute | solution.py:17
  171.1 4.0 %collective-permute-start.10 = (f32[128,256]{0,1:T(8,128)S(1)}, f32[128,256]{0,1:T(8,128)S(1)}, u32[]{:S(2)}, u32[]{:S(2)}) collective-permute-start(f32[128,256]{0,1:T(8,128)S(1)} %get-tuple-element.52), channel_id=1, source_target_pairs={{0,32},{32,64},{64,96},{96,128},{128,160},{160,192},{192,224},{1,3... | collective-permute-start | bytes 393224 | tf_op jit(solution)/shard_map/ppermute | solution.py:17
  179.0 13.1 %collective-permute-start.12 = (f32[128,256]{0,1:T(8,128)S(1)}, f32[128,256]{0,1:T(8,128)S(1)}, u32[]{:S(2)}, u32[]{:S(2)}) collective-permute-start(f32[128,256]{0,1:T(8,128)S(1)} %get-tuple-element.49), channel_id=1, source_target_pairs={{0,1},{1,2},{2,3},{3,4},{4,5},{5,6},{6,7},{7,8},{8,9},{9,10},{10,1... | collective-permute-start | bytes 393224 | tf_op jit(solution)/shard_map/ppermute | solution.py:17
  181.7 12.9 %collective-permute-start.15 = (f32[128,256]{0,1:T(8,128)S(1)}, f32[128,256]{0,1:T(8,128)S(1)}, u32[]{:S(2)}, u32[]{:S(2)}) collective-permute-start(f32[128,256]{0,1:T(8,128)S(1)} %get-tuple-element.47), channel_id=1, source_target_pairs={{32,0},{64,32},{96,64},{128,96},{160,128},{192,160},{224,192},{33,... | collective-permute-start | bytes 393224 | tf_op jit(solution)/shard_map/ppermute | solution.py:17
  183.0 11.6 %collective-permute-start.14 = (f32[128,256]{0,1:T(8,128)S(1)}, f32[128,256]{0,1:T(8,128)S(1)}, u32[]{:S(2)}, u32[]{:S(2)}) collective-permute-start(f32[128,256]{0,1:T(8,128)S(1)} %get-tuple-element.48), channel_id=1, source_target_pairs={{0,32},{32,64},{64,96},{96,128},{128,160},{160,192},{192,224},{1,3... | collective-permute-start | bytes 393224 | tf_op jit(solution)/shard_map/ppermute | solution.py:17
  186.7 7.8 %collective-permute-start.13 = (f32[128,256]{0,1:T(8,128)S(1)}, f32[128,256]{0,1:T(8,128)S(1)}, u32[]{:S(2)}, u32[]{:S(2)}) collective-permute-start(f32[128,256]{0,1:T(8,128)S(1)} %get-tuple-element.50), channel_id=1, source_target_pairs={{1,0},{2,1},{3,2},{4,3},{5,4},{6,5},{7,6},{8,7},{9,8},{10,9},{11,1... | collective-permute-start | bytes 393224 | tf_op jit(solution)/shard_map/ppermute | solution.py:17
  264.8 20.5 %copy-start.3 = (f32[1,1,1024,1024]{3,2,1,0:T(8,128)S(1)}, f32[1,1,1024,1024]{3,2,1,0:T(8,128)}, u32[]{:S(2)}) copy-start(f32[1,1,1024,1024]{3,2,1,0:T(8,128)} %param.6) | copy-start | bytes 12582916
  267.6 36.9 %copy-start.8 = (f32[1024,256]{0,1:T(8,128)}, f32[1024,256]{0,1:T(8,128)S(1)}, u32[]{:S(2)}) copy-start(f32[1024,256]{0,1:T(8,128)S(1)} %fusion.6) | copy-start | bytes 3145732
  267.7 9.0 %collective-permute-start.16 = (f32[128,256]{0,1:T(8,128)S(1)}, f32[128,256]{0,1:T(8,128)S(1)}, u32[]{:S(2)}, u32[]{:S(2)}) collective-permute-start(f32[128,256]{0,1:T(8,128)S(1)} %constant_dynamic-slice_fusion), channel_id=1, source_target_pairs={{0,1},{1,2},{2,3},{3,4},{4,5},{5,6},{6,7},{7,8},{8,9},{9,10},{10,1... | collective-permute-start | bytes 393224 | tf_op jit(solution)/shard_map/ppermute | solution.py:17
  276.7 7.8 %collective-permute-start.17 = (f32[128,256]{0,1:T(8,128)S(1)}, f32[128,256]{0,1:T(8,128)S(1)}, u32[]{:S(2)}, u32[]{:S(2)}) collective-permute-start(f32[128,256]{0,1:T(8,128)S(1)} %get-tuple-element.46), channel_id=1, source_target_pairs={{1,0},{2,1},{3,2},{4,3},{5,4},{6,5},{7,6},{8,7},{9,8},{10,9},{11,1... | collective-permute-start | bytes 393224 | tf_op jit(solution)/shard_map/ppermute | solution.py:17
  279.9 5.3 %collective-permute-start.19 = (f32[128,256]{0,1:T(8,128)S(1)}, f32[128,256]{0,1:T(8,128)S(1)}, u32[]{:S(2)}, u32[]{:S(2)}) collective-permute-start(f32[128,256]{0,1:T(8,128)S(1)} %get-tuple-element.43), channel_id=1, source_target_pairs={{32,0},{64,32},{96,64},{128,96},{160,128},{192,160},{224,192},{33,... | collective-permute-start | bytes 393224 | tf_op jit(solution)/shard_map/ppermute | solution.py:17
  281.2 4.0 %collective-permute-start.18 = (f32[128,256]{0,1:T(8,128)S(1)}, f32[128,256]{0,1:T(8,128)S(1)}, u32[]{:S(2)}, u32[]{:S(2)}) collective-permute-start(f32[128,256]{0,1:T(8,128)S(1)} %get-tuple-element.44), channel_id=1, source_target_pairs={{0,32},{32,64},{64,96},{96,128},{128,160},{160,192},{192,224},{1,3... | collective-permute-start | bytes 393224 | tf_op jit(solution)/shard_map/ppermute | solution.py:17
  289.1 57.1 %copy-start.5 = (f32[1024,256]{0,1:T(8,128)S(1)}, f32[1024,256]{0,1:T(8,128)}, u32[]{:S(2)}) copy-start(f32[1024,256]{0,1:T(8,128)} %copy-done.4) | copy-start | bytes 3145732
  289.2 12.7 %collective-permute-start.20 = (f32[128,256]{0,1:T(8,128)S(1)}, f32[128,256]{0,1:T(8,128)S(1)}, u32[]{:S(2)}, u32[]{:S(2)}) collective-permute-start(f32[128,256]{0,1:T(8,128)S(1)} %get-tuple-element.41), channel_id=1, source_target_pairs={{0,1},{1,2},{2,3},{3,4},{4,5},{5,6},{6,7},{7,8},{8,9},{9,10},{10,1... | collective-permute-start | bytes 393224 | tf_op jit(solution)/shard_map/ppermute | solution.py:17
  292.0 12.5 %collective-permute-start.23 = (f32[128,256]{0,1:T(8,128)S(1)}, f32[128,256]{0,1:T(8,128)S(1)}, u32[]{:S(2)}, u32[]{:S(2)}) collective-permute-start(f32[128,256]{0,1:T(8,128)S(1)} %get-tuple-element.39), channel_id=1, source_target_pairs={{32,0},{64,32},{96,64},{128,96},{160,128},{192,160},{224,192},{33,... | collective-permute-start | bytes 393224 | tf_op jit(solution)/shard_map/ppermute | solution.py:17
  293.3 11.1 %collective-permute-start.22 = (f32[128,256]{0,1:T(8,128)S(1)}, f32[128,256]{0,1:T(8,128)S(1)}, u32[]{:S(2)}, u32[]{:S(2)}) collective-permute-start(f32[128,256]{0,1:T(8,128)S(1)} %get-tuple-element.40), channel_id=1, source_target_pairs={{0,32},{32,64},{64,96},{96,128},{128,160},{160,192},{192,224},{1,3... | collective-permute-start | bytes 393224 | tf_op jit(solution)/shard_map/ppermute | solution.py:17
  296.5 7.8 %collective-permute-start.21 = (f32[128,256]{0,1:T(8,128)S(1)}, f32[128,256]{0,1:T(8,128)S(1)}, u32[]{:S(2)}, u32[]{:S(2)}) collective-permute-start(f32[128,256]{0,1:T(8,128)S(1)} %get-tuple-element.42), channel_id=1, source_target_pairs={{1,0},{2,1},{3,2},{4,3},{5,4},{6,5},{7,6},{8,7},{9,8},{10,9},{11,1... | collective-permute-start | bytes 393224 | tf_op jit(solution)/shard_map/ppermute | solution.py:17
  (6 other events, 50.9 us)
where the time goes:
time: 357 us; the launch traced here: 355 us
  blocking collectives  174 us (49%)
  starting transfers between devices  89.2 us (25%)
  waiting for transfers between devices  39.3 us (11%)
  matrix products  23.3 us (7%)
  local copies, waits for them, and re-layouts  12.8 us (4%)
  other arithmetic  12.7 us (4%)
  between operations  3.99 us (1%)
    psum x12, blocking collectives, one_axis_at_a_time(): x = lax.psum(x, axis)  123 us
    ppermute x24, starting transfers between devices, from_behind(): lax.ppermute(value, axis, [(source, source + steps) for source in range(i...  77.6 us
    all_to_all x2, blocking collectives, copy_for_each(): return lax.all_to_all(copies, axis, split_axis=0, concat_axis=0, tiled=True)  50.9 us
    all_to_all x1, waiting for transfers between devices, copy_for_each(): return lax.all_to_all(copies, axis, split_axis=0, concat_axis=0, tiled=True)  22.2 us
    ppermute x24, waiting for transfers between devices, from_behind(): lax.ppermute(value, axis, [(source, source + steps) for source in range(i...  17.2 us
    all_to_all x1, starting transfers between devices, copy_for_each(): return lax.all_to_all(copies, axis, split_axis=0, concat_axis=0, tiled=True)  11.6 us
    dot_general x3, matrix products, operator(): product = jnp.dot(matrix, inner, precision=lax.Precision.HIGHEST)  11.2 us
    unnamed x35, local copies, waits for them, and re-layouts  8.34 us
  transfers between devices with their start and end apart: 25, of which 10 were waited for; matrix products, arithmetic and copies ran while one was open for 2% of the time, Pallas kernels for 0%

commit v1 on v0

--- a/solution.py
+++ b/solution.py
@@ -35,7 +35,7 @@
 
 def one_axis_at_a_time(x, axes):
     for axis in axes:
-        x = lax.psum(x, axis)
+        x = jnp.sum(lax.all_gather(x, axis), axis=0)
     return x
 
 

time: 357 us -> 439 us (1.23)
  blocking collectives: 174 us -> 255 us
  starting transfers between devices: 89.2 us -> 84.3 us
  waiting for transfers between devices: 39.3 us -> 43.9 us
    all_gather x0 -> x24, blocking collectives: none -> 208 us  [one_axis_at_a_time(): x = jnp.sum(lax.all_gather(x, axis), axis=0)]
    psum x12 -> x0, blocking collectives: 123 us -> none  [one_axis_at_a_time(): x = lax.psum(x, axis)]
    ppermute x24, starting transfers between devices: 77.6 us -> 72.7 us  [from_behind(): lax.ppermute(value, axis, [(source, source + steps) for source in range(i...]
    ppermute x24, waiting for transfers between devices: 17.2 us -> 21.8 us  [from_behind(): lax.ppermute(value, axis, [(source, source + steps) for source in range(i...]
  transfers between devices with their start and end apart: 25 -> 25, of which waited for: 10 -> 12; matrix products, arithmetic and copies ran while one was open for 2% -> 2% of each run, Pallas kernels for 0% -> 0%
where the time goes in v1:
time: 439 us; the launch traced here: 437 us
  blocking collectives  255 us (58%)
  starting transfers between devices  84.3 us (19%)
  waiting for transfers between devices  43.9 us (10%)
  matrix products  23.3 us (5%)
  other arithmetic  13.1 us (3%)
  local copies, waits for them, and re-layouts  12.9 us (3%)
    all_gather x24, blocking collectives, one_axis_at_a_time(): x = jnp.sum(lax.all_gather(x, axis), axis=0)  208 us
    ppermute x24, starting transfers between devices, from_behind(): lax.ppermute(value, axis, [(source, source + steps) for source in range(i...  72.7 us
    all_to_all x2, blocking collectives, copy_for_each(): return lax.all_to_all(copies, axis, split_axis=0, concat_axis=0, tiled=True)  47.4 us
    all_to_all x1, waiting for transfers between devices, copy_for_each(): return lax.all_to_all(copies, axis, split_axis=0, concat_axis=0, tiled=True)  22.1 us
    ppermute x24, waiting for transfers between devices, from_behind(): lax.ppermute(value, axis, [(source, source + steps) for source in range(i...  21.8 us
    all_to_all x1, starting transfers between devices, copy_for_each(): return lax.all_to_all(copies, axis, split_axis=0, concat_axis=0, tiled=True)  11.6 us
    dot_general x3, matrix products, operator(): product = jnp.dot(matrix, inner, precision=lax.Precision.HIGHEST)  11.2 us
  transfers between devices with their start and end apart: 25, of which 12 were waited for; matrix products, arithmetic and copies ran while one was open for 2% of the time, Pallas kernels for 0%

profile of v1, /device:TPU:2, one launch (start us, length us, event | category | flops | bytes accessed | tf_op | source)
XLA Modules:
  0.0 436.9 jit_solution(3555493822034162411)
XLA Ops:
  4.4 11.6 %all-to-all-start = ((f32[32,32,256]{2,1,0:T(8,128)}), f32[32,32,256]{2,1,0:T(8,128)S(1)}, u32[]{:S(2)}, u32[]{:S(2)}) async-start(f32[32,32,256]{2,1,0:T(8,128)} %broadcast_in_dim.10), calls=%async_computation | async-start | bytes 2097152 | tf_op jit(solution)/shard_map/all_to_all | solution.py:22
  20.1 22.1 %all-to-all-done = f32[32,32,256]{2,1,0:T(8,128)S(1)} async-done(((f32[32,32,256]{2,1,0:T(8,128)}), f32[32,32,256]{2,1,0:T(8,128)S(1)}, u32[]{:S(2)}, u32[]{:S(2)}) %all-to-all-start) | async-done | bytes 1048608 | tf_op jit(solution)/shard_map/all_to_all | solution.py:22
  45.0 5.0 %collective-permute-start = (f32[128,256]{0,1:T(8,128)S(1)}, f32[128,256]{0,1:T(8,128)}, u32[]{:S(2)}, u32[]{:S(2)}) collective-permute-start(f32[128,256]{0,1:T(8,128)S(1)} %constant_dynamic-slice_fusion.11), channel_id=1, source_target_pairs={{0,1},{1,2},{2,3},{3,4},{4,5},{5,6},{6,7},{7,8},{8,9},{9,10},{10,1... | collective-permute-start | bytes 393224 | tf_op jit(solution)/shard_map/ppermute | solution.py:17
  72.6 4.4 %collective-permute-start.6 = (f32[128,256]{0,1:T(8,128)S(1)}, f32[128,256]{0,1:T(8,128)S(1)}, u32[]{:S(2)}, u32[]{:S(2)}) collective-permute-start(f32[128,256]{0,1:T(8,128)S(1)} %get-tuple-element.34), channel_id=1, source_target_pairs={{0,32},{32,64},{64,96},{96,128},{128,160},{160,192},{192,224},{1,3... | collective-permute-start | bytes 393224 | tf_op jit(solution)/shard_map/ppermute | solution.py:17
  77.1 4.9 %collective-permute-start.5 = (f32[128,256]{0,1:T(8,128)S(1)}, f32[128,256]{0,1:T(8,128)S(1)}, u32[]{:S(2)}, u32[]{:S(2)}) collective-permute-start(f32[128,256]{0,1:T(8,128)S(1)} %get-tuple-element.36), channel_id=1, source_target_pairs={{1,0},{2,1},{3,2},{4,3},{5,4},{6,5},{7,6},{8,7},{9,8},{10,9},{11,1... | collective-permute-start | bytes 393224 | tf_op jit(solution)/shard_map/ppermute | solution.py:17
  85.0 11.5 %all-gather.24 = f32[4,1,256]{2,1,0:T(1,128)S(1)} all-gather(f32[1,1,256]{2,1,0:T(1,128)S(1)} %bitcast.144), channel_id=2, replica_groups=mesh['cluster_0'=4,'cluster_1'=2,'sub_0'=4,'sub_1'=8] {'cluster_0'}, dimensions={0}, use_global_device_ids=true | all-gather | bytes 5120 | tf_op jit(solution)/shard_map/all_gather | solution.py:38
  98.3 8.0 %all-gather.26 = f32[4,1,256]{2,1,0:T(1,128)S(1)} all-gather(f32[1,1,256]{2,1,0:T(1,128)S(1)} %bitcast.147), channel_id=4, replica_groups=mesh['cluster_0'=4,'cluster_1'=2,'sub_0'=4,'sub_1'=8] {'sub_0'}, dimensions={0}, use_global_device_ids=true | all-gather | bytes 5120 | tf_op jit(solution)/shard_map/all_gather | solution.py:38
  106.3 7.8 %all-gather.28 = f32[4,1,256]{2,1,0:T(1,128)S(1)} all-gather(f32[1,1,256]{2,1,0:T(1,128)S(1)} %bitcast.141), channel_id=6, replica_groups=mesh['cluster_0'=4,'cluster_1'=2,'sub_0'=4,'sub_1'=8] {'cluster_0'}, dimensions={0}, use_global_device_ids=true | all-gather | bytes 5120 | tf_op jit(solution)/shard_map/all_gather | solution.py:38
  116.0 9.2 %all-gather.30 = f32[4,1,256]{2,1,0:T(1,128)S(1)} all-gather(f32[1,1,256]{2,1,0:T(1,128)S(1)} %bitcast.148), channel_id=8, replica_groups=mesh['cluster_0'=4,'cluster_1'=2,'sub_0'=4,'sub_1'=8] {'sub_0'}, dimensions={0}, use_global_device_ids=true | all-gather | bytes 5120 | tf_op jit(solution)/shard_map/all_gather | solution.py:38
  125.2 16.4 %all-gather.31 = f32[8,1,256]{2,1,0:T(1,128)S(1)} all-gather(f32[1,1,256]{2,1,0:T(1,128)S(1)} %bitcast.158), channel_id=9, replica_groups=mesh['cluster_0'=4,'cluster_1'=2,'sub_0'=4,'sub_1'=8] {'sub_1'}, dimensions={0}, use_global_device_ids=true | all-gather | bytes 9216 | tf_op jit(solution)/shard_map/all_gather | solution.py:38
  141.6 13.3 %all-gather.27 = f32[8,1,256]{2,1,0:T(1,128)S(1)} all-gather(f32[1,1,256]{2,1,0:T(1,128)S(1)} %bitcast.153), channel_id=5, replica_groups=mesh['cluster_0'=4,'cluster_1'=2,'sub_0'=4,'sub_1'=8] {'sub_1'}, dimensions={0}, use_global_device_ids=true | all-gather | bytes 9216 | tf_op jit(solution)/shard_map/all_gather | solution.py:38
  157.5 24.2 %all_to_all.15 = f32[32,32,256]{2,1,0:T(8,128)S(1)} all-to-all(f32[32,32,256]{2,1,0:T(8,128)S(1)} %broadcast_in_dim.11), channel_id=1, replica_groups=mesh['cluster_0'=4,'cluster_1'=2,'sub_0'=4,'sub_1'=8] {'sub_0','sub_1'}, dimensions={0} | all-to-all | bytes 2097152 | tf_op jit(solution)/shard_map/all_to_all | solution.py:22
  187.9 5.6 %collective-permute-done.8 = f32[128,256]{0,1:T(8,128)S(1)} collective-permute-done((f32[128,256]{0,1:T(8,128)S(1)}, f32[128,256]{0,1:T(8,128)S(1)}, u32[]{:S(2)}, u32[]{:S(2)}) %collective-permute-start.8) | collective-permute-done | bytes 131104 | tf_op jit(solution)/shard_map/ppermute | solution.py:17
  214.0 4.0 collective-permute-start.13
  222.4 10.5 %all-gather.32 = f32[4,1,256]{2,1,0:T(1,128)S(1)} all-gather(f32[1,1,256]{2,1,0:T(1,128)S(1)} %bitcast.145), channel_id=10, replica_groups=mesh['cluster_0'=4,'cluster_1'=2,'sub_0'=4,'sub_1'=8] {'cluster_0'}, dimensions={0}, use_global_device_ids=true | all-gather | bytes 5120 | tf_op jit(solution)/shard_map/all_gather | solution.py:38
  234.7 8.4 %all-gather.34 = f32[4,1,256]{2,1,0:T(1,128)S(1)} all-gather(f32[1,1,256]{2,1,0:T(1,128)S(1)} %bitcast.149), channel_id=12, replica_groups=mesh['cluster_0'=4,'cluster_1'=2,'sub_0'=4,'sub_1'=8] {'sub_0'}, dimensions={0}, use_global_device_ids=true | all-gather | bytes 5120 | tf_op jit(solution)/shard_map/all_gather | solution.py:38
  243.2 7.4 %all-gather.36 = f32[4,1,256]{2,1,0:T(1,128)S(1)} all-gather(f32[1,1,256]{2,1,0:T(1,128)S(1)} %bitcast.142), channel_id=14, replica_groups=mesh['cluster_0'=4,'cluster_1'=2,'sub_0'=4,'sub_1'=8] {'cluster_0'}, dimensions={0}, use_global_device_ids=true | all-gather | bytes 5120 | tf_op jit(solution)/shard_map/all_gather | solution.py:38
  252.4 9.8 %all-gather.38 = f32[4,1,256]{2,1,0:T(1,128)S(1)} all-gather(f32[1,1,256]{2,1,0:T(1,128)S(1)} %bitcast.150), channel_id=16, replica_groups=mesh['cluster_0'=4,'cluster_1'=2,'sub_0'=4,'sub_1'=8] {'sub_0'}, dimensions={0}, use_global_device_ids=true | all-gather | bytes 5120 | tf_op jit(solution)/shard_map/all_gather | solution.py:38
  262.3 15.8 %all-gather.39 = f32[8,1,256]{2,1,0:T(1,128)S(1)} all-gather(f32[1,1,256]{2,1,0:T(1,128)S(1)} %bitcast.161), channel_id=17, replica_groups=mesh['cluster_0'=4,'cluster_1'=2,'sub_0'=4,'sub_1'=8] {'sub_1'}, dimensions={0}, use_global_device_ids=true | all-gather | bytes 9216 | tf_op jit(solution)/shard_map/all_gather | solution.py:38
  278.1 13.3 %all-gather.35 = f32[8,1,256]{2,1,0:T(1,128)S(1)} all-gather(f32[1,1,256]{2,1,0:T(1,128)S(1)} %bitcast.154), channel_id=13, replica_groups=mesh['cluster_0'=4,'cluster_1'=2,'sub_0'=4,'sub_1'=8] {'sub_1'}, dimensions={0}, use_global_device_ids=true | all-gather | bytes 9216 | tf_op jit(solution)/shard_map/all_gather | solution.py:38
  294.0 23.1 %all_to_all.16 = f32[32,32,256]{2,1,0:T(8,128)S(1)} all-to-all(f32[32,32,256]{2,1,0:T(8,128)S(1)} %broadcast_in_dim.12), channel_id=1, replica_groups=mesh['cluster_0'=4,'cluster_1'=2,'sub_0'=4,'sub_1'=8] {'sub_0','sub_1'}, dimensions={0} | all-to-all | bytes 2097152 | tf_op jit(solution)/shard_map/all_to_all | solution.py:22
  324.0 5.0 %collective-permute-done.16 = f32[128,256]{0,1:T(8,128)S(1)} collective-permute-done((f32[128,256]{0,1:T(8,128)S(1)}, f32[128,256]{0,1:T(8,128)S(1)}, u32[]{:S(2)}, u32[]{:S(2)}) %collective-permute-start.16) | collective-permute-done | bytes 131104 | tf_op jit(solution)/shard_map/ppermute | solution.py:17
  340.5 4.1 collective-permute-start.20
  345.8 4.4 %collective-permute-start.22 = (f32[128,256]{0,1:T(8,128)S(1)}, f32[128,256]{0,1:T(8,128)S(1)}, u32[]{:S(2)}, u32[]{:S(2)}) collective-permute-start(f32[128,256]{0,1:T(8,128)S(1)} %get-tuple-element.18), channel_id=1, source_target_pairs={{0,32},{32,64},{64,96},{96,128},{128,160},{160,192},{192,224},{1,3... | collective-permute-start | bytes 393224 | tf_op jit(solution)/shard_map/ppermute | solution.py:17
  350.3 4.0 collective-permute-start.21
  358.3 10.5 %all-gather.40 = f32[4,1,256]{2,1,0:T(1,128)S(1)} all-gather(f32[1,1,256]{2,1,0:T(1,128)S(1)} %bitcast.146), channel_id=18, replica_groups=mesh['cluster_0'=4,'cluster_1'=2,'sub_0'=4,'sub_1'=8] {'cluster_0'}, dimensions={0}, use_global_device_ids=true | all-gather | bytes 5120 | tf_op jit(solution)/shard_map/all_gather | solution.py:38
  370.6 8.8 %all-gather.42 = f32[4,1,256]{2,1,0:T(1,128)S(1)} all-gather(f32[1,1,256]{2,1,0:T(1,128)S(1)} %bitcast.151), channel_id=20, replica_groups=mesh['cluster_0'=4,'cluster_1'=2,'sub_0'=4,'sub_1'=8] {'sub_0'}, dimensions={0}, use_global_device_ids=true | all-gather | bytes 5120 | tf_op jit(solution)/shard_map/all_gather | solution.py:38
  379.4 7.4 %all-gather.44 = f32[4,1,256]{2,1,0:T(1,128)S(1)} all-gather(f32[1,1,256]{2,1,0:T(1,128)S(1)} %bitcast.143), channel_id=22, replica_groups=mesh['cluster_0'=4,'cluster_1'=2,'sub_0'=4,'sub_1'=8] {'cluster_0'}, dimensions={0}, use_global_device_ids=true | all-gather | bytes 5120 | tf_op jit(solution)/shard_map/all_gather | solution.py:38
  388.6 9.6 %all-gather.46 = f32[4,1,256]{2,1,0:T(1,128)S(1)} all-gather(f32[1,1,256]{2,1,0:T(1,128)S(1)} %bitcast.152), channel_id=24, replica_groups=mesh['cluster_0'=4,'cluster_1'=2,'sub_0'=4,'sub_1'=8] {'sub_0'}, dimensions={0}, use_global_device_ids=true | all-gather | bytes 5120 | tf_op jit(solution)/shard_map/all_gather | solution.py:38
  398.2 16.1 %all-gather.47 = f32[8,1,256]{2,1,0:T(1,128)S(1)} all-gather(f32[1,1,256]{2,1,0:T(1,128)S(1)} %bitcast.164), channel_id=25, replica_groups=mesh['cluster_0'=4,'cluster_1'=2,'sub_0'=4,'sub_1'=8] {'sub_1'}, dimensions={0}, use_global_device_ids=true | all-gather | bytes 9216 | tf_op jit(solution)/shard_map/all_gather | solution.py:38
  414.3 13.3 %all-gather.43 = f32[8,1,256]{2,1,0:T(1,128)S(1)} all-gather(f32[1,1,256]{2,1,0:T(1,128)S(1)} %bitcast.155), channel_id=21, replica_groups=mesh['cluster_0'=4,'cluster_1'=2,'sub_0'=4,'sub_1'=8] {'sub_1'}, dimensions={0}, use_global_device_ids=true | all-gather | bytes 9216 | tf_op jit(solution)/shard_map/all_gather | solution.py:38
  427.7 4.1 subtract_bitcast_fusion
  (164 shorter events, 109.0 us)
Async XLA Ops:
  0.7 41.5 %copy-start.12 = (f32[1,32,1024]{2,1,0:T(8,128)S(1)}, f32[1,32,1024]{2,1,0:T(8,128)}, u32[]{:S(2)}) copy-start(f32[1,32,1024]{2,1,0:T(8,128)} %param.9) | copy-start | bytes 393220
  4.4 37.7 %all-to-all-start = ((f32[32,32,256]{2,1,0:T(8,128)}), f32[32,32,256]{2,1,0:T(8,128)S(1)}, u32[]{:S(2)}, u32[]{:S(2)}) async-start(f32[32,32,256]{2,1,0:T(8,128)} %broadcast_in_dim.10), calls=%async_computation | async-start | bytes 2097152 | tf_op jit(solution)/shard_map/all_to_all | solution.py:22
  16.4 68.2 %copy-start.9 = (f32[1,1,1024,256]{2,3,1,0:T(8,128)}, f32[1,1,1024,256]{2,3,1,0:T(8,128)S(1)}, u32[]{:S(2)}) copy-start(f32[1,1,1024,256]{2,3,1,0:T(8,128)S(1)} %copy.11) | copy-start | bytes 3145732
  44.9 39.7 %copy-start.6 = (f32[1024,256]{0,1:T(8,128)}, f32[1024,256]{0,1:T(8,128)S(1)}, u32[]{:S(2)}) copy-start(f32[1024,256]{0,1:T(8,128)S(1)} %fusion.8) | copy-start | bytes 3145732
  45.0 9.1 %collective-permute-start = (f32[128,256]{0,1:T(8,128)S(1)}, f32[128,256]{0,1:T(8,128)}, u32[]{:S(2)}, u32[]{:S(2)}) collective-permute-start(f32[128,256]{0,1:T(8,128)S(1)} %constant_dynamic-slice_fusion.11), channel_id=1, source_target_pairs={{0,1},{1,2},{2,3},{3,4},{4,5},{5,6},{6,7},{7,8},{8,9},{9,10},{10,1... | collective-permute-start | bytes 393224 | tf_op jit(solution)/shard_map/ppermute | solution.py:17
  55.0 8.4 %collective-permute-start.1 = (f32[128,256]{0,1:T(8,128)S(1)}, f32[128,256]{0,1:T(8,128)S(1)}, u32[]{:S(2)}, u32[]{:S(2)}) collective-permute-start(f32[128,256]{0,1:T(8,128)S(1)} %get-tuple-element.40), channel_id=1, source_target_pairs={{1,0},{2,1},{3,2},{4,3},{5,4},{6,5},{7,6},{8,7},{9,8},{10,9},{11,1... | collective-permute-start | bytes 393224 | tf_op jit(solution)/shard_map/ppermute | solution.py:17
  59.0 5.3 %collective-permute-start.3 = (f32[128,256]{0,1:T(8,128)S(1)}, f32[128,256]{0,1:T(8,128)S(1)}, u32[]{:S(2)}, u32[]{:S(2)}) collective-permute-start(f32[128,256]{0,1:T(8,128)S(1)} %get-tuple-element.37), channel_id=1, source_target_pairs={{32,0},{64,32},{96,64},{128,96},{160,128},{192,160},{224,192},{33,... | collective-permute-start | bytes 393224 | tf_op jit(solution)/shard_map/ppermute | solution.py:17
  60.3 4.0 collective-permute-start.2
  68.3 13.8 %collective-permute-start.4 = (f32[128,256]{0,1:T(8,128)S(1)}, f32[128,256]{0,1:T(8,128)S(1)}, u32[]{:S(2)}, u32[]{:S(2)}) collective-permute-start(f32[128,256]{0,1:T(8,128)S(1)} %get-tuple-element.35), channel_id=1, source_target_pairs={{0,1},{1,2},{2,3},{3,4},{4,5},{5,6},{6,7},{7,8},{8,9},{9,10},{10,1... | collective-permute-start | bytes 393224 | tf_op jit(solution)/shard_map/ppermute | solution.py:17
  71.3 13.2 %collective-permute-start.7 = (f32[128,256]{0,1:T(8,128)S(1)}, f32[128,256]{0,1:T(8,128)S(1)}, u32[]{:S(2)}, u32[]{:S(2)}) collective-permute-start(f32[128,256]{0,1:T(8,128)S(1)} %get-tuple-element.33), channel_id=1, source_target_pairs={{32,0},{64,32},{96,64},{128,96},{160,128},{192,160},{224,192},{33,... | collective-permute-start | bytes 393224 | tf_op jit(solution)/shard_map/ppermute | solution.py:17
  72.6 11.9 %collective-permute-start.6 = (f32[128,256]{0,1:T(8,128)S(1)}, f32[128,256]{0,1:T(8,128)S(1)}, u32[]{:S(2)}, u32[]{:S(2)}) collective-permute-start(f32[128,256]{0,1:T(8,128)S(1)} %get-tuple-element.34), channel_id=1, source_target_pairs={{0,32},{32,64},{64,96},{96,128},{128,160},{160,192},{192,224},{1,3... | collective-permute-start | bytes 393224 | tf_op jit(solution)/shard_map/ppermute | solution.py:17
  77.1 7.4 %collective-permute-start.5 = (f32[128,256]{0,1:T(8,128)S(1)}, f32[128,256]{0,1:T(8,128)S(1)}, u32[]{:S(2)}, u32[]{:S(2)}) collective-permute-start(f32[128,256]{0,1:T(8,128)S(1)} %get-tuple-element.36), channel_id=1, source_target_pairs={{1,0},{2,1},{3,2},{4,3},{5,4},{6,5},{7,6},{8,7},{9,8},{10,9},{11,1... | collective-permute-start | bytes 393224 | tf_op jit(solution)/shard_map/ppermute | solution.py:17
  184.5 36.5 %copy-start.7 = (f32[1024,256]{0,1:T(8,128)}, f32[1024,256]{0,1:T(8,128)S(1)}, u32[]{:S(2)}) copy-start(f32[1024,256]{0,1:T(8,128)S(1)} %fusion.7) | copy-start | bytes 3145732
  184.5 9.0 %collective-permute-start.8 = (f32[128,256]{0,1:T(8,128)S(1)}, f32[128,256]{0,1:T(8,128)S(1)}, u32[]{:S(2)}, u32[]{:S(2)}) collective-permute-start(f32[128,256]{0,1:T(8,128)S(1)} %constant_dynamic-slice_fusion.4), channel_id=1, source_target_pairs={{0,1},{1,2},{2,3},{3,4},{4,5},{5,6},{6,7},{7,8},{8,9},{9,10},{10,1... | collective-permute-start | bytes 393224 | tf_op jit(solution)/shard_map/ppermute | solution.py:17
  193.6 6.9 %collective-permute-start.9 = (f32[128,256]{0,1:T(8,128)S(1)}, f32[128,256]{0,1:T(8,128)S(1)}, u32[]{:S(2)}, u32[]{:S(2)}) collective-permute-start(f32[128,256]{0,1:T(8,128)S(1)} %get-tuple-element.32), channel_id=1, source_target_pairs={{1,0},{2,1},{3,2},{4,3},{5,4},{6,5},{7,6},{8,7},{9,8},{10,9},{11,1... | collective-permute-start | bytes 393224 | tf_op jit(solution)/shard_map/ppermute | solution.py:17
  195.5 5.3 %collective-permute-start.11 = (f32[128,256]{0,1:T(8,128)S(1)}, f32[128,256]{0,1:T(8,128)S(1)}, u32[]{:S(2)}, u32[]{:S(2)}) collective-permute-start(f32[128,256]{0,1:T(8,128)S(1)} %get-tuple-element.29), channel_id=1, source_target_pairs={{32,0},{64,32},{96,64},{128,96},{160,128},{192,160},{224,192},{33,... | collective-permute-start | bytes 393224 | tf_op jit(solution)/shard_map/ppermute | solution.py:17
  196.8 4.0 collective-permute-start.10
  204.7 13.4 %collective-permute-start.12 = (f32[128,256]{0,1:T(8,128)S(1)}, f32[128,256]{0,1:T(8,128)S(1)}, u32[]{:S(2)}, u32[]{:S(2)}) collective-permute-start(f32[128,256]{0,1:T(8,128)S(1)} %get-tuple-element.27), channel_id=1, source_target_pairs={{0,1},{1,2},{2,3},{3,4},{4,5},{5,6},{6,7},{7,8},{8,9},{9,10},{10,1... | collective-permute-start | bytes 393224 | tf_op jit(solution)/shard_map/ppermute | solution.py:17
  208.7 12.3 %collective-permute-start.15 = (f32[128,256]{0,1:T(8,128)S(1)}, f32[128,256]{0,1:T(8,128)S(1)}, u32[]{:S(2)}, u32[]{:S(2)}) collective-permute-start(f32[128,256]{0,1:T(8,128)S(1)} %get-tuple-element.25), channel_id=1, source_target_pairs={{32,0},{64,32},{96,64},{128,96},{160,128},{192,160},{224,192},{33,... | collective-permute-start | bytes 393224 | tf_op jit(solution)/shard_map/ppermute | solution.py:17
  210.0 10.9 %collective-permute-start.14 = (f32[128,256]{0,1:T(8,128)S(1)}, f32[128,256]{0,1:T(8,128)S(1)}, u32[]{:S(2)}, u32[]{:S(2)}) collective-permute-start(f32[128,256]{0,1:T(8,128)S(1)} %get-tuple-element.26), channel_id=1, source_target_pairs={{0,32},{32,64},{64,96},{96,128},{128,160},{160,192},{192,224},{1,3... | collective-permute-start | bytes 393224 | tf_op jit(solution)/shard_map/ppermute | solution.py:17
  214.0 6.9 %collective-permute-start.13 = (f32[128,256]{0,1:T(8,128)S(1)}, f32[128,256]{0,1:T(8,128)S(1)}, u32[]{:S(2)}, u32[]{:S(2)}) collective-permute-start(f32[128,256]{0,1:T(8,128)S(1)} %get-tuple-element.28), channel_id=1, source_target_pairs={{1,0},{2,1},{3,2},{4,3},{5,4},{6,5},{7,6},{8,7},{9,8},{10,9},{11,1... | collective-permute-start | bytes 393224 | tf_op jit(solution)/shard_map/ppermute | solution.py:17
  317.2 19.4 %copy-start.3 = (f32[1,1,1024,1024]{3,2,1,0:T(8,128)S(1)}, f32[1,1,1024,1024]{3,2,1,0:T(8,128)}, u32[]{:S(2)}) copy-start(f32[1,1,1024,1024]{3,2,1,0:T(8,128)} %param.6) | copy-start | bytes 12582916
  320.0 37.3 %copy-start.8 = (f32[1024,256]{0,1:T(8,128)}, f32[1024,256]{0,1:T(8,128)S(1)}, u32[]{:S(2)}) copy-start(f32[1024,256]{0,1:T(8,128)S(1)} %fusion.6) | copy-start | bytes 3145732
  320.0 9.0 %collective-permute-start.16 = (f32[128,256]{0,1:T(8,128)S(1)}, f32[128,256]{0,1:T(8,128)S(1)}, u32[]{:S(2)}, u32[]{:S(2)}) collective-permute-start(f32[128,256]{0,1:T(8,128)S(1)} %constant_dynamic-slice_fusion), channel_id=1, source_target_pairs={{0,1},{1,2},{2,3},{3,4},{4,5},{5,6},{6,7},{7,8},{8,9},{9,10},{10,1... | collective-permute-start | bytes 393224 | tf_op jit(solution)/shard_map/ppermute | solution.py:17
  329.1 6.9 %collective-permute-start.17 = (f32[128,256]{0,1:T(8,128)S(1)}, f32[128,256]{0,1:T(8,128)S(1)}, u32[]{:S(2)}, u32[]{:S(2)}) collective-permute-start(f32[128,256]{0,1:T(8,128)S(1)} %get-tuple-element.24), channel_id=1, source_target_pairs={{1,0},{2,1},{3,2},{4,3},{5,4},{6,5},{7,6},{8,7},{9,8},{10,9},{11,1... | collective-permute-start | bytes 393224 | tf_op jit(solution)/shard_map/ppermute | solution.py:17
  331.2 5.3 %collective-permute-start.19 = (f32[128,256]{0,1:T(8,128)S(1)}, f32[128,256]{0,1:T(8,128)S(1)}, u32[]{:S(2)}, u32[]{:S(2)}) collective-permute-start(f32[128,256]{0,1:T(8,128)S(1)} %get-tuple-element.21), channel_id=1, source_target_pairs={{32,0},{64,32},{96,64},{128,96},{160,128},{192,160},{224,192},{33,... | collective-permute-start | bytes 393224 | tf_op jit(solution)/shard_map/ppermute | solution.py:17
  332.5 4.0 collective-permute-start.18
  340.4 87.3 %copy-start.5 = (f32[1024,256]{0,1:T(8,128)S(1)}, f32[1024,256]{0,1:T(8,128)}, u32[]{:S(2)}) copy-start(f32[1024,256]{0,1:T(8,128)} %copy-done.4) | copy-start | bytes 3145732
  340.5 13.9 %collective-permute-start.20 = (f32[128,256]{0,1:T(8,128)S(1)}, f32[128,256]{0,1:T(8,128)S(1)}, u32[]{:S(2)}, u32[]{:S(2)}) collective-permute-start(f32[128,256]{0,1:T(8,128)S(1)} %get-tuple-element.19), channel_id=1, source_target_pairs={{0,1},{1,2},{2,3},{3,4},{4,5},{5,6},{6,7},{7,8},{8,9},{9,10},{10,1... | collective-permute-start | bytes 393224 | tf_op jit(solution)/shard_map/ppermute | solution.py:17
  344.5 12.7 %collective-permute-start.23 = (f32[128,256]{0,1:T(8,128)S(1)}, f32[128,256]{0,1:T(8,128)S(1)}, u32[]{:S(2)}, u32[]{:S(2)}) collective-permute-start(f32[128,256]{0,1:T(8,128)S(1)} %get-tuple-element.17), channel_id=1, source_target_pairs={{32,0},{64,32},{96,64},{128,96},{160,128},{192,160},{224,192},{33,... | collective-permute-start | bytes 393224 | tf_op jit(solution)/shard_map/ppermute | solution.py:17
  345.8 11.4 %collective-permute-start.22 = (f32[128,256]{0,1:T(8,128)S(1)}, f32[128,256]{0,1:T(8,128)S(1)}, u32[]{:S(2)}, u32[]{:S(2)}) collective-permute-start(f32[128,256]{0,1:T(8,128)S(1)} %get-tuple-element.18), channel_id=1, source_target_pairs={{0,32},{32,64},{64,96},{96,128},{128,160},{160,192},{192,224},{1,3... | collective-permute-start | bytes 393224 | tf_op jit(solution)/shard_map/ppermute | solution.py:17
  350.3 6.9 %collective-permute-start.21 = (f32[128,256]{0,1:T(8,128)S(1)}, f32[128,256]{0,1:T(8,128)S(1)}, u32[]{:S(2)}, u32[]{:S(2)}) collective-permute-start(f32[128,256]{0,1:T(8,128)S(1)} %get-tuple-element.20), channel_id=1, source_target_pairs={{1,0},{2,1},{3,2},{4,3},{5,4},{6,5},{7,6},{8,7},{9,8},{10,9},{11,1... | collective-permute-start | bytes 393224 | tf_op jit(solution)/shard_map/ppermute | solution.py:17
  (6 other events, 49.5 us)
